TPU v7x, 32 devices: a whole 2x2x4 slice. The times are simulated.
32 devices in a mesh: ctx: 8 (over z, y), head: 4 (over x, core).
Axes of the slice: x: 2, y: 2, z: 4, core: 2. Of those that a mesh axis runs over, the one named last changes fastest.
Arguments:
- queries: bfloat16 [1024, 64, 576], P('ctx', 'head'), may hold values from -100 to 100
- latent_cache: bfloat16 [16, 36864], P('ctx'), may hold values from -6 to 6
- selected: int32 [16, 8], P('ctx'), may hold values from -1 to 15, as said below
- value_weight: bfloat16 [64, 512, 128], P('head'), may hold values from -0.25 to 0.25
Outputs:
- attended: bfloat16 [1024, 8192], P(('ctx', 'head'))
Inputs may be any that keep to these rules, and one draw needn't show every extreme that they name: `selected`: row b lists distinct key blocks: its first entry is b itself, the others lie below b; where b + 1 < 8 the row holds all of 0 to b and its remaining slots are -1.
All inputs are finite; a program needn't handle non-finite values.
Results may differ from a plain program's by a relative error of at most 0.011.
Values may be sent and summed in bfloat16 or wider, within the bound.
A program may use at most 64 MiB of HBM per device.

v0:
```python
import jax
import jax.numpy as jnp
from jax import lax
from jax.sharding import PartitionSpec as P

DC = 512
DR = 64
DV = 128
KBLK = 64
SEL = 8


def attend_block(query_rows, key_rows, chosen_ids, block_index, value_weight):
    score_scale = (DV + DR) ** (-0.5)
    offsets = jnp.arange(KBLK, dtype=jnp.int32)
    valid_slot = chosen_ids >= 0
    clipped = jnp.maximum(chosen_ids, 0)
    key_place = (clipped[:, None] * KBLK + offsets[None, :]).reshape(-1)
    key_valid = jnp.repeat(valid_slot, KBLK)
    query_place = block_index * KBLK + offsets
    scores = (
        jnp.einsum("qhc,kc->hqk", query_rows, key_rows, preferred_element_type=jnp.float32)
        * score_scale
    )
    allowed = key_valid[None, None, :] & (key_place[None, None, :] <= query_place[None, :, None])
    scores = jnp.where(allowed, scores, -1e30)
    largest = jnp.max(scores, axis=2, keepdims=True)
    powered = jnp.exp(scores - largest)
    weights = (powered / jnp.sum(powered, axis=2, keepdims=True)).astype(jnp.bfloat16)
    mixed_latent = jnp.einsum(
        "hqk,kc->qhc", weights, key_rows[:, :DC], preferred_element_type=jnp.float32
    ).astype(jnp.bfloat16)
    expanded = jnp.einsum(
        "qhc,hcv->qhv", mixed_latent, value_weight, preferred_element_type=jnp.float32
    )
    return expanded.astype(jnp.bfloat16).reshape(KBLK, -1)


def per_device(queries, latent_cache, selected, value_weight):
    latent_width = DC + DR
    blocks_here = selected.shape[0]
    ctx_size = lax.axis_size("ctx")
    slice_width = latent_cache.shape[1] // ctx_size
    spread = lax.all_to_all(
        latent_cache.reshape(blocks_here, ctx_size, slice_width),
        "ctx",
        split_axis=1,
        concat_axis=0,
        tiled=True,
    )
    banded = spread.reshape(blocks_here * ctx_size, slice_width)
    every_choice = lax.all_gather(selected, "ctx", axis=0, tiled=True)
    clipped_all = jnp.maximum(every_choice, 0)
    pieces = banded[clipped_all].reshape(ctx_size, blocks_here, SEL, slice_width)
    fetched = lax.all_to_all(pieces, "ctx", split_axis=0, concat_axis=3, tiled=True)
    key_blocks = fetched.reshape(blocks_here, SEL * KBLK, latent_width)
    base_block = lax.axis_index("ctx") * blocks_here

    def one_block(position):
        query_rows = lax.dynamic_slice_in_dim(queries, position * KBLK, KBLK, 0)
        return attend_block(
            query_rows,
            key_blocks[position],
            selected[position],
            base_block + position,
            value_weight,
        )

    attended_here = lax.map(one_block, jnp.arange(blocks_here, dtype=jnp.int32))
    attended_here = attended_here.reshape(blocks_here * KBLK, -1)
    return lax.all_to_all(attended_here, "head", split_axis=0, concat_axis=1, tiled=True)


def solution(mesh):
    in_specs = (P("ctx", "head", None), P("ctx", None), P("ctx", None), P("head", None, None))
    out_specs = P(("ctx", "head"), None)
    return jax.shard_map(
        per_device, mesh=mesh, in_specs=in_specs, out_specs=out_specs, check_vma=False
    )
```

profile of v0, /device:TPU:0, one launch (start us, length us, event | category | flops | bytes accessed | tf_op | source)
XLA Modules:
  0.0 100.5 jit_solution(3366466175248134381)
XLA Ops:
  0.0 7.3 %all-to-all-start = ((bf16[2,8,4608]{2,0,1:T(2,128)(2,1)}), bf16[2,8,4608]{2,0,1:T(2,128)(2,1)S(1)}, u32[]{:S(2)}, u32[]{:S(2)}) async-start(bf16[2,8,4608]{2,0,1:T(2,128)(2,1)} %bitcast.71), calls=%async_computation | async-start | bytes 294912 | tf_op jit(solution)/shard_map/all_to_all | solution.py:44
  7.3 21.2 %all-gather = s32[8,2,8]{2,1,0:T(2,128)S(1)} all-gather(s32[1,2,8]{2,1,0:T(2,128)} %bitcast.72), channel_id=1, replica_groups=mesh['ctx'=8,'head'=4] {'ctx'}, dimensions={0}, use_global_device_ids=true | all-gather | bytes 576 | tf_op jit(solution)/shard_map/all_gather | solution.py:52
  28.5 0.1 reshape.116
  28.6 0.0 all-to-all-done
  28.6 0.1 reshape.111
  28.7 2.3 %gather_fusion = bf16[128,4608]{1,0:T(8,128)(2,1)} fusion(bf16[16,4608]{1,0:T(8,128)(2,1)S(1)} %reshape.111, s32[1024]{0:T(1024)S(1)} %pad_clamp_fusion), kind=kCustom, calls=%fused_computation | custom fusion | bytes 2359808 | tf_op jit(solution)/shard_map/gather | solution.py:54
  31.0 0.0 copy-start
  31.0 3.7 %all-to-all-start.1 = ((bf16[8,2,8,4608]{3,2,1,0:T(8,128)(2,1)}), bf16[8,2,8,4608]{3,2,1,0:T(8,128)(2,1)S(1)}, u32[]{:S(2)}, u32[]{:S(2)}) async-start(bf16[8,2,8,4608]{3,2,1,0:T(8,128)(2,1)} %bitcast.12), calls=%async_computation.1 | async-start | bytes 2359296 | tf_op jit(solution)/shard_map/all_to_all | solution.py:55
  34.7 0.0 copy-done
  34.7 2.5 %copy.25 = bf16[128,16,576]{2,0,1:T(8,128)(2,1)} copy(bf16[128,16,576]{0,2,1:T(8,128)(2,1)S(1)} %copy-done) | data formatting | bytes 4718592 | tf_op jit(solution)/shard_map/while | solution.py:69
  37.3 22.1 %all-to-all-done.1 = bf16[8,2,8,4608]{3,2,1,0:T(8,128)(2,1)S(1)} async-done(((bf16[8,2,8,4608]{3,2,1,0:T(8,128)(2,1)}), bf16[8,2,8,4608]{3,2,1,0:T(8,128)(2,1)S(1)}, u32[]{:S(2)}, u32[]{:S(2)}) %all-to-all-start.1) | async-done | bytes 1179680 | tf_op jit(solution)/shard_map/all_to_all | solution.py:55
  59.4 1.7 %copy.23 = bf16[1,2,8,8,4608]{4,3,2,1,0:T(8,128)(2,1)} copy(bf16[1,2,8,8,4608]{4,2,1,3,0:T(8,128)(2,1)S(1)} %bitcast.67) | data formatting | bytes 2359296 | tf_op jit(solution)/shard_map/all_to_all | solution.py:55
  61.0 0.0 copy-start.1
  61.1 0.0 copy-start.2
  61.1 2.7 %reshape.113 = bf16[2,512,576]{2,1,0:T(8,128)(2,1)S(1)} reshape(bf16[1,2,8,8,4608]{4,3,2,1,0:T(8,128)(2,1)} %copy.23) | data formatting | bytes 2359296 | tf_op jit(solution)/shard_map/reshape | solution.py:56
  63.7 0.6 copy.24
  64.4 0.0 copy-done.1
  64.4 0.0 copy-done.2
  64.4 23.8 %while.10 = (s32[]{:T(128)}, bf16[2,64,2048]{2,1,0:T(8,128)(2,1)S(1)}, s32[2]{0:T(128)S(1)}, bf16[2,512,576]{1,2,0:T(8,128)(2,1)S(1)}, s32[2,8]{1,0:T(2,128)S(1)...) while((s32[]{:T(128)}, ...), condition=%wide.region_3.4_spmd, body=%wide.region_0.3_spmd.sunk | while | flops 1278936192 | bytes 11819933 | solution.py:69
  64.4 0.6 dynamic_slice.52
  67.0 0.1 iota_add_fusion.4
  67.0 0.1 add.67
  67.1 0.1 broadcast_in_dim.52
  67.2 0.1 and.23
  67.9 0.1 compare_and_fusion.2
  68.7 4.0 %fusion.43 = (f32[16,64]{1,0:T(8,128)S(1)}, f32[16,64,512]{2,1,0:T(8,128)}) fusion(pred[64,512]{1,0:T(8,128)(4,1)S(1)} %compare_and_fusion.2, bf16[128,16,576]{2,0,1:T(8,128)(2,1)} %get-tuple-element.183, s32[]{:T(128)S(6)} %select_n.23, bf16[2,512,576]{1,2,0:T(8,128)(2,1)S(1)} %get-tuple-element.180, s32[]{:T(128)S(6)} %select_n.22), kind=kOutput, calls=%fused_computation.32.clone.1 | convolution fusion | flops 606077440 | bytes 4034568 | tf_op jit(solution)/shard_map/while/body/eval_jaxpr/sub | solution.py:28
  72.7 3.3 %fusion.44 = bf16[64,16,128]{2,0,1:T(8,128)(2,1)S(1)} fusion(bf16[16,512,128]{2,1,0:T(8,128)(2,1)} %get-tuple-element.184, f32[16,64,512]{2,1,0:T(8,128)} %get-tuple-element.149, f32[16,64]{1,0:T(8,128)S(1)} %get-tuple-element.150, bf16[512,576]{0,1:T(8,128)(2,1)S(1)} %dynamic-slice_bitcast_fusion.2), kind=kOutput, calls=%fused_computation.11.clone.1 | convolution fusion | flops 672792576 | bytes 4988928 | tf_op jit(solution)/shard_map/while/body/eval_jaxpr/qhc,hcv->qhv/dot_general | solution.py:33
  76.0 0.2 copy.31
  76.2 0.1 broadcast_in_dim.53
  76.3 0.6 dynamic_slice.52
  78.9 0.1 iota_add_fusion.4
  79.0 0.1 add.67
  79.0 0.1 broadcast_in_dim.52
  79.1 0.1 and.23
  79.9 0.1 compare_and_fusion.2
  80.6 4.0 %fusion.43 = (f32[16,64]{1,0:T(8,128)S(1)}, f32[16,64,512]{2,1,0:T(8,128)}) fusion(pred[64,512]{1,0:T(8,128)(4,1)S(1)} %compare_and_fusion.2, bf16[128,16,576]{2,0,1:T(8,128)(2,1)} %get-tuple-element.183, s32[]{:T(128)S(6)} %select_n.23, bf16[2,512,576]{1,2,0:T(8,128)(2,1)S(1)} %get-tuple-element.180, s32[]{:T(128)S(6)} %select_n.22), kind=kOutput, calls=%fused_computation.32.clone.1 | convolution fusion | flops 606077440 | bytes 4034568 | tf_op jit(solution)/shard_map/while/body/eval_jaxpr/sub | solution.py:28
  84.6 3.3 %fusion.44 = bf16[64,16,128]{2,0,1:T(8,128)(2,1)S(1)} fusion(bf16[16,512,128]{2,1,0:T(8,128)(2,1)} %get-tuple-element.184, f32[16,64,512]{2,1,0:T(8,128)} %get-tuple-element.149, f32[16,64]{1,0:T(8,128)S(1)} %get-tuple-element.150, bf16[512,576]{0,1:T(8,128)(2,1)S(1)} %dynamic-slice_bitcast_fusion.2), kind=kOutput, calls=%fused_computation.11.clone.1 | convolution fusion | flops 672792576 | bytes 4988928 | tf_op jit(solution)/shard_map/while/body/eval_jaxpr/qhc,hcv->qhv/dot_general | solution.py:33
  87.9 0.2 copy.31
  88.1 0.1 broadcast_in_dim.53
  88.2 11.4 %all_to_all.49 = bf16[4,32,2048]{2,1,0:T(8,128)(2,1)S(1)} all-to-all(bf16[4,32,2048]{2,1,0:T(8,128)(2,1)S(1)} %bitcast.70), channel_id=1, replica_groups=mesh['ctx'=8,'head'=4] {'head'}, dimensions={0} | all-to-all | bytes 1048576 | tf_op jit(solution)/shard_map/all_to_all | solution.py:71
  99.6 0.8 copy.29
  (14 shorter events, 0.2 us)
Async XLA Ops:
  0.0 28.6 %all-to-all-start = ((bf16[2,8,4608]{2,0,1:T(2,128)(2,1)}), bf16[2,8,4608]{2,0,1:T(2,128)(2,1)S(1)}, u32[]{:S(2)}, u32[]{:S(2)}) async-start(bf16[2,8,4608]{2,0,1:T(2,128)(2,1)} %bitcast.71), calls=%async_computation | async-start | bytes 294912 | tf_op jit(solution)/shard_map/all_to_all | solution.py:44
  31.0 3.7 %copy-start = (bf16[128,16,576]{0,2,1:T(8,128)(2,1)S(1)}, bf16[128,16,576]{0,2,1:T(8,128)(2,1)}, u32[]{:S(2)}) copy-start(bf16[128,16,576]{0,2,1:T(8,128)(2,1)} %param.6) | copy-start | bytes 7077892
  31.0 28.3 %all-to-all-start.1 = ((bf16[8,2,8,4608]{3,2,1,0:T(8,128)(2,1)}), bf16[8,2,8,4608]{3,2,1,0:T(8,128)(2,1)S(1)}, u32[]{:S(2)}, u32[]{:S(2)}) async-start(bf16[8,2,8,4608]{3,2,1,0:T(8,128)(2,1)} %bitcast.12), calls=%async_computation.1 | async-start | bytes 2359296 | tf_op jit(solution)/shard_map/all_to_all | solution.py:55
  61.0 3.3 %copy-start.1 = (bf16[2,64,2048]{2,1,0:T(8,128)(2,1)S(1)}, bf16[2,64,2048]{2,1,0:T(8,128)(2,1)}, u32[]{:S(2)}) copy-start(bf16[2,64,2048]{2,1,0:T(8,128)(2,1)} %custom-call.2) | copy-start | bytes 1572868
  61.1 3.3 %copy-start.2 = (s32[2,8]{1,0:T(2,128)S(1)}, s32[2,8]{1,0:T(2,128)}, u32[]{:S(2)}) copy-start(s32[2,8]{1,0:T(2,128)} %param.8) | copy-start | bytes 196
where the time goes:
time: 101 us; the launch traced here: 100 us
  blocking collectives  32.6 us (32%)
  waiting for transfers between devices  22.1 us (22%)
  matrix products  14.5 us (14%)
  local copies, waits for them, and re-layouts  13.2 us (13%)
  starting transfers between devices  11 us (11%)
  loops' own time  6.64 us (7%)
    all_to_all x1, waiting for transfers between devices, per_device(): lax.all_to_all(pieces, 'ctx', split_axis=0, concat_axis=3, tiled=True)  22.1 us
    all_gather x1, blocking collectives, per_device(): every_choice = lax.all_gather(selected, 'ctx', axis=0, tiled=True)  21.2 us
    all_to_all x1, blocking collectives, per_device(): lax.all_to_all(attended_here, 'head', split_axis=0, concat_axis=1, tiled=...  11.4 us
    sub x2, matrix products, attend_block(): powered = jnp.exp(scores - largest)  7.92 us
    all_to_all x1, starting transfers between devices, per_device(): lax.all_to_all(latent_cache.reshape(blocks_here, ctx_size, slice_width),...  7.28 us
    another operation x1, loops' own time, per_device(): attended_here = lax.map(one_block, jnp.arange(blocks_here, dtype=jnp.int32))  6.64 us
    dot_general x2, matrix products, attend_block(): jnp.einsum('qhc,hcv->qhv', mixed_latent, value_weight, preferred_element_...  6.55 us
    all_to_all x1, starting transfers between devices, per_device(): lax.all_to_all(pieces, 'ctx', split_axis=0, concat_axis=3, tiled=True)  3.69 us
  transfers between devices with their start and end apart: 2, of which 1 were waited for; matrix products, arithmetic and copies ran while one was open for 3% of the time, Pallas kernels for 0%

commit v1 on v0

v1 whole, which is shorter than its diff:
```python
import functools
import math

import jax
import jax.numpy as jnp
from jax import lax
from jax.experimental import pallas as pl
from jax.experimental.pallas import tpu as pltpu
from jax.sharding import PartitionSpec as P

DC = 512
DR = 64
DV = 128
KBLK = 64
SEL = 8
GROUPS = 4
MESH = pl.DeviceIdType.MESH
FAR = 1 << 30


def kernel(
    n_ctx, n_head, heads,
    sel_ref, own_ref, q_hbm, w_hbm, out_ref,
    keys, kbuf, q_ref, q_blocks, w_ref, stage,
    load_sem, s1, r1, s2, r2, s3, r3, s4, r4, s_out, r_out, l_out,
):
    c = lax.axis_index("ctx")
    h = lax.axis_index("head")
    x, core = h // 2, h % 2
    h_core = 2 * x + (1 - core)
    h_x = 2 * (1 - x) + core
    h_diag = 2 * (1 - x) + (1 - core)
    own_rows = own_ref.shape[0]
    blocks = own_rows // KBLK
    part = own_rows // n_head

    load_q = pltpu.make_async_copy(q_hbm, q_ref, load_sem.at[0])
    load_w = pltpu.make_async_copy(w_hbm, w_ref, load_sem.at[1])
    load_q.start()
    load_w.start()

    barrier = pltpu.get_barrier_semaphore()
    for peer in (h_core, h_x, h_diag):
        pl.semaphore_signal(barrier, inc=1, device_id=(c, peer), device_id_type=MESH)

    @pl.loop(0, c)
    def _(lower):
        pl.semaphore_signal(barrier, inc=1, device_id=(lower, h), device_id_type=MESH)

    pl.semaphore_wait(barrier, 3 + n_ctx - 1 - c)

    def piece(source, quarter):
        row = quarter * part
        start = pl.multiple_of(row % KBLK, part)
        return keys.at[source * blocks + row // KBLK, pl.ds(start, part), :]

    def first_copy(source, target):
        return pltpu.make_async_remote_copy(
            src_ref=own_ref.at[pl.ds(pl.multiple_of(h * part, part), part), :],
            dst_ref=piece(source, h),
            send_sem=s1.at[target], recv_sem=r1.at[source],
            device_id=(target, h), device_id_type=MESH,
        )

    def relay(source, quarter, peer, send, recv):
        return pltpu.make_async_remote_copy(
            src_ref=piece(source, quarter), dst_ref=piece(source, quarter),
            send_sem=send.at[source], recv_sem=recv.at[source],
            device_id=(c, peer), device_id_type=MESH,
        )

    @pl.loop(0, n_ctx - 1 - c)
    def _(step):
        first_copy(c, n_ctx - 1 - step).start()

    for block in range(blocks):
        keys[c * blocks + block] = own_ref[block * KBLK:(block + 1) * KBLK, :]

    @pl.loop(0, c + 1)
    def _(step):
        @pl.when(step < c)
        def _():
            source = c - 1 - step
            first_copy(source, c).wait_recv()
            relay(source, h, h_x, s2, r2).start()
            relay(source, h, h_core, s3, r3).start()

        @pl.when(step > 0)
        def _():
            source = c - step
            relay(source, h_x, h_x, s2, r2).wait_recv()
            relay(source, h_x, h_core, s4, r4).start()

    load_q.wait()
    for pair in range(heads // 2):
        group, slot = divmod(pair, heads // (2 * GROUPS))
        lanes = slice(slot * 2 * KBLK, (slot + 1) * 2 * KBLK)
        first, second = q_ref[2 * pair], q_ref[2 * pair + 1]
        q_blocks[0, group, :, lanes] = jnp.concatenate([first[:, :KBLK], second[:, :KBLK]], axis=1)
        q_blocks[1, group, :, lanes] = jnp.concatenate([first[:, KBLK:], second[:, KBLK:]], axis=1)
    load_w.wait()

    @pl.loop(0, c)
    def _(step):
        source = c - 1 - step
        relay(source, h_core, h_core, s3, r3).wait_recv()
        relay(source, h_diag, h_core, s4, r4).wait_recv()

    factor = (DV + DR) ** (-0.5) * math.log2(math.e)
    key_row = lax.broadcasted_iota(jnp.int32, (SEL * KBLK, 1), 0)
    per_group = heads // GROUPS
    width = per_group * DV
    columns = per_group * KBLK
    token = lax.broadcasted_iota(jnp.int32, (1, columns), 1) % KBLK

    def out_copy(group, target, relation):
        return pltpu.make_async_remote_copy(
            src_ref=stage.at[target, :, pl.ds(group * width, width)],
            dst_ref=out_ref.at[:, pl.ds(pl.multiple_of(h * (heads * DV) + group * width, width), width)],
            send_sem=s_out.at[relation, group], recv_sem=r_out.at[relation, group],
            device_id=(c, target), device_id_type=MESH,
        )

    def out_local(group):
        return pltpu.make_async_copy(
            stage.at[h, :, pl.ds(group * width, width)],
            out_ref.at[:, pl.ds(pl.multiple_of(h * (heads * DV) + group * width, width), width)],
            l_out.at[group],
        )

    half = KBLK // 2
    for turn in range(2):
        position = (1 - x) if turn == 0 else x
        key_block = jnp.zeros((SEL * KBLK, 1), jnp.int32)
        for slot in range(SEL):
            chosen = sel_ref[position, slot]
            kbuf[slot * KBLK:(slot + 1) * KBLK, :] = keys[jnp.maximum(chosen, 0)]
            key_block = jnp.where(key_row // KBLK == slot, chosen, key_block)
        key_place = jnp.where(key_block < 0, FAR, key_block * KBLK + key_row % KBLK)

        query_place = token + (c * blocks + position) * KBLK
        for group in range(GROUPS):
            query = q_blocks[position, group]
            scores = jnp.dot(kbuf[...], query, preferred_element_type=jnp.float32)
            scores = jnp.where(key_place <= query_place, scores, -1e30)
            largest = jnp.max(scores, axis=0, keepdims=True)
            powered = jnp.exp2((scores - largest) * factor)
            total = jnp.sum(powered, axis=0, keepdims=True)
            weights = (powered * (1.0 / total)).astype(jnp.bfloat16)
            latent = jnp.dot(
                weights.T, kbuf[:, :DC], preferred_element_type=jnp.float32
            ).astype(jnp.bfloat16)
            for inner in range(per_group):
                head = group * per_group + inner
                value = jnp.dot(
                    latent[inner * KBLK:(inner + 1) * KBLK], w_ref[head], preferred_element_type=jnp.float32
                ).astype(jnp.bfloat16)
                stage[2 * position, :, head * DV:(head + 1) * DV] = value[:half]
                stage[2 * position + 1, :, head * DV:(head + 1) * DV] = value[half:]
            if turn == 0:
                out_copy(group, h_x, 0).start()
                out_copy(group, h_diag, 1).start()
            else:
                out_copy(group, h_core, 2).start()
                out_local(group).start()

    for group in range(GROUPS):
        out_local(group).wait()
        for relation, peer in enumerate((h_x, h_diag, h_core)):
            out_copy(group, peer, relation).wait()

    @pl.loop(0, n_ctx - 1 - c)
    def _(step):
        first_copy(c, n_ctx - 1 - step).wait_send()

    @pl.loop(0, c)
    def _(source):
        relay(source, h, h_x, s2, r2).wait_send()
        relay(source, h, h_core, s3, r3).wait_send()
        relay(source, h_x, h_core, s4, r4).wait_send()


def per_device(queries, latent_cache, selected, value_weight):
    n_ctx, n_head = lax.axis_size("ctx"), lax.axis_size("head")
    width = DC + DR
    tokens, heads = queries.shape[:2]
    own = latent_cache.reshape(tokens, width)
    by_head = queries.transpose(1, 2, 0)
    part = tokens // n_head
    dma = pltpu.SemaphoreType.DMA
    return pl.pallas_call(
        functools.partial(kernel, n_ctx, n_head, heads),
        out_shape=jax.ShapeDtypeStruct((part, n_head * heads * DV), jnp.bfloat16),
        in_specs=[
            pl.BlockSpec(memory_space=pltpu.SMEM),
            pl.BlockSpec(memory_space=pltpu.VMEM),
            pl.BlockSpec(memory_space=pl.ANY),
            pl.BlockSpec(memory_space=pl.ANY),
        ],
        out_specs=pl.BlockSpec(memory_space=pl.ANY),
        scratch_shapes=[
            pltpu.VMEM((n_ctx * tokens // KBLK, KBLK, width), jnp.bfloat16),
            pltpu.VMEM((SEL * KBLK, width), jnp.bfloat16),
            pltpu.VMEM((heads, width, tokens), jnp.bfloat16),
            pltpu.VMEM((tokens // KBLK, GROUPS, width, heads // GROUPS * KBLK), jnp.bfloat16),
            pltpu.VMEM((heads, DC, DV), jnp.bfloat16),
            pltpu.VMEM((n_head, part, heads * DV), jnp.bfloat16),
            dma((2,)),
            dma((n_ctx,)), dma((n_ctx,)),
            dma((n_ctx,)), dma((n_ctx,)),
            dma((n_ctx,)), dma((n_ctx,)),
            dma((n_ctx,)), dma((n_ctx,)),
            dma((3, GROUPS)), dma((3, GROUPS)), dma((GROUPS,)),
        ],
        compiler_params=pltpu.CompilerParams(
            collective_id=0, has_side_effects=True, vmem_limit_bytes=52 * 1024 * 1024
        ),
    )(selected, own, by_head, value_weight)


def solution(mesh):
    in_specs = (P("ctx", "head", None), P("ctx", None), P("ctx", None), P("head", None, None))
    out_specs = P(("ctx", "head"), None)
    return jax.shard_map(
        per_device, mesh=mesh, in_specs=in_specs, out_specs=out_specs, check_vma=False
    )
```

time: 101 us -> 35.2 us (0.35)
  the two profiles are of different devices: /device:TPU:0 before, /device:TPU:17 now
where the time goes in v1:
time: 35.2 us; the launch traced here: 34.5 us
  Pallas kernels  31.9 us (91%)
  local copies, waits for them, and re-layouts  2.58 us (7%)
    pallas_call x1, Pallas kernels, per_device(): pl.pallas_call(functools.partial(kernel, n_ctx, n_head, heads), out_shape...  31.9 us
    unnamed x3, local copies, waits for them, and re-layouts  1.47 us
    reshape x1, local copies, waits for them, and re-layouts, per_device(): own = latent_cache.reshape(tokens, width)  1.1 us

profile of v1, /device:TPU:17, one launch (start us, length us, event | category | flops | bytes accessed | tf_op | source)
XLA Modules:
  0.0 34.5 jit_solution(10929719536464810798)
XLA Ops:
  0.0 1.1 %reshape.3.own_ref = bf16[128,576]{1,0:T(8,128)(2,1)S(1)} reshape(bf16[2,36864]{1,0:T(2,128)(2,1)} %param.5) | data formatting | bytes 294912 | tf_op jit(solution)/shard_map/reshape | solution.py:187
  1.1 0.0 copy-start
  1.1 0.7 %copy-done = s32[2,8]{1,0:T(2,128)S(1)} copy-done((s32[2,8]{1,0:T(2,128)S(1)}, s32[2,8]{1,0:T(2,128)}, u32[]{:S(2)}) %copy-start) | copy-done | bytes 88
  1.8 31.9 %shard_map.46 = bf16[32,8192]{1,0:T(8,128)(2,1)S(1)} custom-call(s32[2,8]{1,0:T(2,128)S(1)} %copy-done, bf16[128,576]{1,0:T(8,128)(2,1)S(1)} %reshape.3.own_ref, bf16[16,576,128]{2,1,0:T(8,128)(2,1)} %bitcast.1, bf16[16,512,128]{2,1,0:T(8,128)(2,1)} %w_hbm.1), custom_call_target="tpu_custom_call" | custom-call | tf_op jit(solution)/shard_map/pallas_call | solution.py:191
  33.7 0.8 %copy.6 = bf16[32,8192]{1,0:T(8,128)(2,1)} copy(bf16[32,8192]{1,0:T(8,128)(2,1)S(1)} %shard_map.46) | data formatting | bytes 1048576
Async XLA Ops:
  1.1 0.7 %copy-start = (s32[2,8]{1,0:T(2,128)S(1)}, s32[2,8]{1,0:T(2,128)}, u32[]{:S(2)}) copy-start(s32[2,8]{1,0:T(2,128)} %sel_ref.1) | copy-start | bytes 196

commit v2 on v1

--- a/solution.py
+++ b/solution.py
@@ -14,14 +14,17 @@
 KBLK = 64
 SEL = 8
 GROUPS = 4
+LAG_RELAY = 2
+LAG_SCORE = 4
+DENSE_BLOCKS = 32
 MESH = pl.DeviceIdType.MESH
 FAR = 1 << 30
 
 
 def kernel(
-    n_ctx, n_head, heads,
-    sel_ref, own_ref, q_hbm, w_hbm, out_ref,
-    keys, kbuf, q_ref, q_blocks, w_ref, stage,
+    n_ctx, n_head, heads, dense,
+    sel_hbm, own_ref, q_hbm, w_hbm, out_ref,
+    sel_ref, keys, kbuf, q_ref, q_blocks, scored, w_ref, stage,
     load_sem, s1, r1, s2, r2, s3, r3, s4, r4, s_out, r_out, l_out,
 ):
     c = lax.axis_index("ctx")
@@ -36,7 +39,9 @@
 
     load_q = pltpu.make_async_copy(q_hbm, q_ref, load_sem.at[0])
     load_w = pltpu.make_async_copy(w_hbm, w_ref, load_sem.at[1])
+    load_sel = pltpu.make_async_copy(sel_hbm, sel_ref, load_sem.at[2])
     load_q.start()
+    load_sel.start()
     load_w.start()
 
     barrier = pltpu.get_barrier_semaphore()
@@ -76,7 +81,28 @@
     for block in range(blocks):
         keys[c * blocks + block] = own_ref[block * KBLK:(block + 1) * KBLK, :]
 
-    @pl.loop(0, c + 1)
+    load_q.wait()
+    per_group = heads // GROUPS
+    columns = per_group * KBLK
+    for pair in range(heads // 2):
+        group, slot = divmod(pair, heads // (2 * GROUPS))
+        lanes = slice(slot * 2 * KBLK, (slot + 1) * 2 * KBLK)
+        first, second = q_ref[2 * pair], q_ref[2 * pair + 1]
+        q_blocks[0, group, :, lanes] = jnp.concatenate([first[:, :KBLK], second[:, :KBLK]], axis=1)
+        q_blocks[1, group, :, lanes] = jnp.concatenate([first[:, KBLK:], second[:, KBLK:]], axis=1)
+
+    def score_source(source):
+        rows = jnp.concatenate([keys[source * blocks + block] for block in range(blocks)], axis=0)
+        for position in range(2):
+            for group in range(GROUPS):
+                result = jnp.dot(rows, q_blocks[position, group], preferred_element_type=jnp.float32)
+                for block in range(blocks):
+                    scored[source * blocks + block, position, group] = result[block * KBLK:(block + 1) * KBLK]
+
+    if dense:
+        score_source(c)
+
+    @pl.loop(0, c + LAG_SCORE)
     def _(step):
         @pl.when(step < c)
         def _():
@@ -85,32 +111,26 @@
             relay(source, h, h_x, s2, r2).start()
             relay(source, h, h_core, s3, r3).start()
 
-        @pl.when(step > 0)
+        @pl.when((step >= LAG_RELAY) & (step < c + LAG_RELAY))
         def _():
-            source = c - step
+            source = c - 1 - (step - LAG_RELAY)
             relay(source, h_x, h_x, s2, r2).wait_recv()
             relay(source, h_x, h_core, s4, r4).start()
 
-    load_q.wait()
-    for pair in range(heads // 2):
-        group, slot = divmod(pair, heads // (2 * GROUPS))
-        lanes = slice(slot * 2 * KBLK, (slot + 1) * 2 * KBLK)
-        first, second = q_ref[2 * pair], q_ref[2 * pair + 1]
-        q_blocks[0, group, :, lanes] = jnp.concatenate([first[:, :KBLK], second[:, :KBLK]], axis=1)
-        q_blocks[1, group, :, lanes] = jnp.concatenate([first[:, KBLK:], second[:, KBLK:]], axis=1)
+        @pl.when(step >= LAG_SCORE)
+        def _():
+            source = c - 1 - (step - LAG_SCORE)
+            relay(source, h_core, h_core, s3, r3).wait_recv()
+            relay(source, h_diag, h_core, s4, r4).wait_recv()
+            if dense:
+                score_source(source)
+
     load_w.wait()
-
-    @pl.loop(0, c)
-    def _(step):
-        source = c - 1 - step
-        relay(source, h_core, h_core, s3, r3).wait_recv()
-        relay(source, h_diag, h_core, s4, r4).wait_recv()
+    load_sel.wait()
 
     factor = (DV + DR) ** (-0.5) * math.log2(math.e)
     key_row = lax.broadcasted_iota(jnp.int32, (SEL * KBLK, 1), 0)
-    per_group = heads // GROUPS
     width = per_group * DV
-    columns = per_group * KBLK
     token = lax.broadcasted_iota(jnp.int32, (1, columns), 1) % KBLK
 
     def out_copy(group, target, relation):
@@ -129,40 +149,60 @@
         )
 
     half = KBLK // 2
+
+    def slots_of(position):
+        chosen = [sel_ref[position, slot] for slot in range(SEL)]
+        return chosen, [jnp.maximum(one, 0) for one in chosen]
+
+    def weigh(position, group):
+        chosen, entry = slots_of(position)
+        key_block = jnp.full((SEL * KBLK, 1), chosen[0], jnp.int32)
+        for slot in range(1, SEL):
+            key_block = jnp.where(key_row // KBLK == slot, chosen[slot], key_block)
+        key_place = jnp.where(key_block < 0, FAR, key_block * KBLK + key_row % KBLK)
+        query_place = token + (c * blocks + position) * KBLK
+        if dense:
+            scores = jnp.concatenate([scored[one, position, group] for one in entry], axis=0)
+        else:
+            rows = jnp.concatenate([keys[one] for one in entry], axis=0)
+            scores = jnp.dot(rows, q_blocks[position, group], preferred_element_type=jnp.float32)
+        scores = jnp.where(key_place <= query_place, scores, -1e30)
+        largest = jnp.max(scores, axis=0, keepdims=True)
+        powered = jnp.exp2((scores - largest) * factor)
+        total = jnp.sum(powered, axis=0, keepdims=True)
+        return (powered * (1.0 / total)).astype(jnp.bfloat16).T
+
+    def finish(turn, position, group, weights):
+        latent = jnp.dot(weights, kbuf[turn], preferred_element_type=jnp.float32).astype(jnp.bfloat16)
+        for inner in range(per_group):
+            head = group * per_group + inner
+            value = jnp.dot(
+                latent[inner * KBLK:(inner + 1) * KBLK], w_ref[head], preferred_element_type=jnp.float32
+            ).astype(jnp.bfloat16)
+            stage[2 * position, :, head * DV:(head + 1) * DV] = value[:half]
+            stage[2 * position + 1, :, head * DV:(head + 1) * DV] = value[half:]
+
+    def send(turn, group):
+        if turn == 0:
+            out_copy(group, h_x, 0).start()
+            out_copy(group, h_diag, 1).start()
+        else:
+            out_copy(group, h_core, 2).start()
+            out_local(group).start()
+
+    order = [(turn, (1 - x) if turn == 0 else x, group) for turn in range(2) for group in range(GROUPS)]
     for turn in range(2):
-        position = (1 - x) if turn == 0 else x
-        key_block = jnp.zeros((SEL * KBLK, 1), jnp.int32)
+        _, entry = slots_of((1 - x) if turn == 0 else x)
         for slot in range(SEL):
-            chosen = sel_ref[position, slot]
-            kbuf[slot * KBLK:(slot + 1) * KBLK, :] = keys[jnp.maximum(chosen, 0)]
-            key_block = jnp.where(key_row // KBLK == slot, chosen, key_block)
-        key_place = jnp.where(key_block < 0, FAR, key_block * KBLK + key_row % KBLK)
-
-        query_place = token + (c * blocks + position) * KBLK
-        for group in range(GROUPS):
-            query = q_blocks[position, group]
-            scores = jnp.dot(kbuf[...], query, preferred_element_type=jnp.float32)
-            scores = jnp.where(key_place <= query_place, scores, -1e30)
-            largest = jnp.max(scores, axis=0, keepdims=True)
-            powered = jnp.exp2((scores - largest) * factor)
-            total = jnp.sum(powered, axis=0, keepdims=True)
-            weights = (powered * (1.0 / total)).astype(jnp.bfloat16)
-            latent = jnp.dot(
-                weights.T, kbuf[:, :DC], preferred_element_type=jnp.float32
-            ).astype(jnp.bfloat16)
-            for inner in range(per_group):
-                head = group * per_group + inner
-                value = jnp.dot(
-                    latent[inner * KBLK:(inner + 1) * KBLK], w_ref[head], preferred_element_type=jnp.float32
-                ).astype(jnp.bfloat16)
-                stage[2 * position, :, head * DV:(head + 1) * DV] = value[:half]
-                stage[2 * position + 1, :, head * DV:(head + 1) * DV] = value[half:]
-            if turn == 0:
-                out_copy(group, h_x, 0).start()
-                out_copy(group, h_diag, 1).start()
-            else:
-                out_copy(group, h_core, 2).start()
-                out_local(group).start()
+            kbuf[turn, slot * KBLK:(slot + 1) * KBLK, :] = keys[entry[slot], :, :DC]
+    weights = weigh(order[0][1], order[0][2])
+    for number, (turn, position, group) in enumerate(order):
+        after = None
+        if number + 1 < len(order):
+            after = weigh(order[number + 1][1], order[number + 1][2])
+        finish(turn, position, group, weights)
+        send(turn, group)
+        weights = after
 
     for group in range(GROUPS):
         out_local(group).wait()
@@ -187,25 +227,30 @@
     own = latent_cache.reshape(tokens, width)
     by_head = queries.transpose(1, 2, 0)
     part = tokens // n_head
+    n_blocks = n_ctx * tokens // KBLK
+    dense = n_blocks <= DENSE_BLOCKS
+    scored_blocks = n_blocks if dense else 1
     dma = pltpu.SemaphoreType.DMA
     return pl.pallas_call(
-        functools.partial(kernel, n_ctx, n_head, heads),
+        functools.partial(kernel, n_ctx, n_head, heads, dense),
         out_shape=jax.ShapeDtypeStruct((part, n_head * heads * DV), jnp.bfloat16),
         in_specs=[
-            pl.BlockSpec(memory_space=pltpu.SMEM),
+            pl.BlockSpec(memory_space=pltpu.HBM),
             pl.BlockSpec(memory_space=pltpu.VMEM),
             pl.BlockSpec(memory_space=pl.ANY),
             pl.BlockSpec(memory_space=pl.ANY),
         ],
         out_specs=pl.BlockSpec(memory_space=pl.ANY),
         scratch_shapes=[
+            pltpu.SMEM(selected.shape, jnp.int32),
             pltpu.VMEM((n_ctx * tokens // KBLK, KBLK, width), jnp.bfloat16),
-            pltpu.VMEM((SEL * KBLK, width), jnp.bfloat16),
+            pltpu.VMEM((2, SEL * KBLK, DC), jnp.bfloat16),
             pltpu.VMEM((heads, width, tokens), jnp.bfloat16),
             pltpu.VMEM((tokens // KBLK, GROUPS, width, heads // GROUPS * KBLK), jnp.bfloat16),
+            pltpu.VMEM((scored_blocks, 2, GROUPS, KBLK, heads // GROUPS * KBLK), jnp.float32),
             pltpu.VMEM((heads, DC, DV), jnp.bfloat16),
             pltpu.VMEM((n_head, part, heads * DV), jnp.bfloat16),
-            dma((2,)),
+            dma((3,)),
             dma((n_ctx,)), dma((n_ctx,)),
             dma((n_ctx,)), dma((n_ctx,)),
             dma((n_ctx,)), dma((n_ctx,)),

time: 35.2 us -> 31.7 us (0.901); the launches traced: 34.5 us -> 31.5 us
  Pallas kernels: 31.9 us -> 29 us
    pallas_call x1, Pallas kernels: 31.9 us -> 29 us  [per_device(): pl.pallas_call(functools.partial(kernel, n_ctx, n_head, heads, dense), ou...]
where the time goes in v2:
time: 31.7 us; the launch traced here: 31.5 us
  Pallas kernels  29 us (91%)
  local copies, waits for them, and re-layouts  2.58 us (8%)
    pallas_call x1, Pallas kernels, per_device(): pl.pallas_call(functools.partial(kernel, n_ctx, n_head, heads, dense), ou...  29 us
    unnamed x3, local copies, waits for them, and re-layouts  1.47 us
    reshape x1, local copies, waits for them, and re-layouts, per_device(): own = latent_cache.reshape(tokens, width)  1.1 us

profile of v2, /device:TPU:17, one launch (start us, length us, event | category | flops | bytes accessed | tf_op | source)
XLA Modules:
  0.0 31.5 jit_solution(9280432517603108785)
XLA Ops:
  0.0 1.1 %reshape.3.own_ref = bf16[128,576]{1,0:T(8,128)(2,1)S(1)} reshape(bf16[2,36864]{1,0:T(2,128)(2,1)} %param.5) | data formatting | bytes 294912 | tf_op jit(solution)/shard_map/reshape | solution.py:227
  1.1 0.0 copy-start
  1.1 0.7 %copy-done = s32[2,8]{1,0:T(2,128)S(1)} copy-done((s32[2,8]{1,0:T(2,128)S(1)}, s32[2,8]{1,0:T(2,128)}, u32[]{:S(2)}) %copy-start) | copy-done | bytes 88
  1.8 29.0 %shard_map.46 = bf16[32,8192]{1,0:T(8,128)(2,1)S(1)} custom-call(s32[2,8]{1,0:T(2,128)S(1)} %copy-done, bf16[128,576]{1,0:T(8,128)(2,1)S(1)} %reshape.3.own_ref, bf16[16,576,128]{2,1,0:T(8,128)(2,1)} %bitcast.1, bf16[16,512,128]{2,1,0:T(8,128)(2,1)} %w_hbm.1), custom_call_target="tpu_custom_call" | custom-call | tf_op jit(solution)/shard_map/pallas_call | solution.py:234
  30.8 0.8 %copy.6 = bf16[32,8192]{1,0:T(8,128)(2,1)} copy(bf16[32,8192]{1,0:T(8,128)(2,1)S(1)} %shard_map.46) | data formatting | bytes 1048576
Async XLA Ops:
  1.1 0.7 %copy-start = (s32[2,8]{1,0:T(2,128)S(1)}, s32[2,8]{1,0:T(2,128)}, u32[]{:S(2)}) copy-start(s32[2,8]{1,0:T(2,128)} %sel_hbm.1) | copy-start | bytes 196

commit v3 on v2

--- a/solution.py
+++ b/solution.py
@@ -14,8 +14,6 @@
 KBLK = 64
 SEL = 8
 GROUPS = 4
-LAG_RELAY = 2
-LAG_SCORE = 4
 DENSE_BLOCKS = 32
 MESH = pl.DeviceIdType.MESH
 FAR = 1 << 30
@@ -25,10 +23,12 @@
     n_ctx, n_head, heads, dense,
     sel_hbm, own_ref, q_hbm, w_hbm, out_ref,
     sel_ref, keys, kbuf, q_ref, q_blocks, scored, w_ref, stage,
-    load_sem, s1, r1, s2, r2, s3, r3, s4, r4, s_out, r_out, l_out,
+    load_sem, s_pair, s_side, s1, r1, s2, r2, s3, r3, s4, r4, s_out, r_out, l_out,
 ):
     c = lax.axis_index("ctx")
     h = lax.axis_index("head")
+    plane, side = c // 2, c % 2
+    c_pair = 2 * plane + (1 - side)
     x, core = h // 2, h % 2
     h_core = 2 * x + (1 - core)
     h_x = 2 * (1 - x) + core
@@ -48,11 +48,14 @@
     for peer in (h_core, h_x, h_diag):
         pl.semaphore_signal(barrier, inc=1, device_id=(c, peer), device_id_type=MESH)
 
-    @pl.loop(0, c)
+    pl.semaphore_signal(barrier, inc=1, device_id=(c_pair, h), device_id_type=MESH)
+
+    @pl.loop(0, plane)
     def _(lower):
-        pl.semaphore_signal(barrier, inc=1, device_id=(lower, h), device_id_type=MESH)
-
-    pl.semaphore_wait(barrier, 3 + n_ctx - 1 - c)
+        pl.semaphore_signal(barrier, inc=1, device_id=(2 * lower + side, h), device_id_type=MESH)
+
+    above = n_ctx // 2 - 1 - plane
+    pl.semaphore_wait(barrier, 4 + above)
 
     def piece(source, quarter):
         row = quarter * part
@@ -67,6 +70,21 @@
             device_id=(target, h), device_id_type=MESH,
         )
 
+    def pair_copy(source, quarter, send, recv):
+        return pltpu.make_async_remote_copy(
+            src_ref=own_ref.at[pl.ds(pl.multiple_of(quarter * part, part), part), :],
+            dst_ref=piece(source, quarter),
+            send_sem=s_pair.at[send], recv_sem=recv.at[source],
+            device_id=(c_pair, h), device_id_type=MESH,
+        )
+
+    def side_copy(source):
+        return pltpu.make_async_remote_copy(
+            src_ref=piece(source, h), dst_ref=piece(source, h),
+            send_sem=s_side.at[source], recv_sem=r1.at[source],
+            device_id=(c_pair, h), device_id_type=MESH,
+        )
+
     def relay(source, quarter, peer, send, recv):
         return pltpu.make_async_remote_copy(
             src_ref=piece(source, quarter), dst_ref=piece(source, quarter),
@@ -74,9 +92,14 @@
             device_id=(c, peer), device_id_type=MESH,
         )
 
-    @pl.loop(0, n_ctx - 1 - c)
+    @pl.when(side == 0)
+    def _():
+        pair_copy(c, h, 0, r1).start()
+        pair_copy(c, h_x, 1, r2).start()
+
+    @pl.loop(0, above)
     def _(step):
-        first_copy(c, n_ctx - 1 - step).start()
+        first_copy(c, n_ctx - 2 + side - 2 * step).start()
 
     for block in range(blocks):
         keys[c * blocks + block] = own_ref[block * KBLK:(block + 1) * KBLK, :]
@@ -99,31 +122,70 @@
                 for block in range(blocks):
                     scored[source * blocks + block, position, group] = result[block * KBLK:(block + 1) * KBLK]
 
-    if dense:
-        score_source(c)
-
-    @pl.loop(0, c + LAG_SCORE)
+    def pass_on(source, across):
+        first_copy(source, c).wait_recv()
+        relay(source, h, h_core, s3, r3).start()
+
+        if across is True:
+            relay(source, h, h_x, s2, r2).start()
+        else:
+            @pl.when(across)
+            def _():
+                relay(source, h, h_x, s2, r2).start()
+
+    def pass_second(source):
+        relay(source, h_x, h_x, s2, r2).wait_recv()
+        relay(source, h_x, h_core, s4, r4).start()
+
+    def complete(source):
+        relay(source, h_core, h_core, s3, r3).wait_recv()
+        relay(source, h_diag, h_core, s4, r4).wait_recv()
+        if dense:
+            score_source(source)
+
+    def same(step):
+        return 2 * (plane - 1 - step) + side
+
+    def other(step):
+        return 2 * (plane - step) + (1 - side)
+
+    def has_same(step):
+        return (step >= 0) & (step < plane)
+
+    def has_other(step):
+        return (step >= 1 - side) & (step <= plane)
+
+    @pl.loop(0, plane + 3)
     def _(step):
-        @pl.when(step < c)
-        def _():
-            source = c - 1 - step
-            first_copy(source, c).wait_recv()
-            relay(source, h, h_x, s2, r2).start()
-            relay(source, h, h_core, s3, r3).start()
-
-        @pl.when((step >= LAG_RELAY) & (step < c + LAG_RELAY))
-        def _():
-            source = c - 1 - (step - LAG_RELAY)
-            relay(source, h_x, h_x, s2, r2).wait_recv()
-            relay(source, h_x, h_core, s4, r4).start()
-
-        @pl.when(step >= LAG_SCORE)
-        def _():
-            source = c - 1 - (step - LAG_SCORE)
-            relay(source, h_core, h_core, s3, r3).wait_recv()
-            relay(source, h_diag, h_core, s4, r4).wait_recv()
-            if dense:
-                score_source(source)
+        @pl.when(has_same(step))
+        def _():
+            pass_on(same(step), True)
+            side_copy(same(step)).start()
+
+        @pl.when(has_other(step))
+        def _():
+            pass_on(other(step), step > 0)
+
+        if dense:
+            @pl.when(step == 0)
+            def _():
+                score_source(c)
+
+        @pl.when(has_same(step - 1))
+        def _():
+            pass_second(same(step - 1))
+
+        @pl.when(has_other(step - 1))
+        def _():
+            pass_second(other(step - 1))
+
+        @pl.when(has_same(step - 2))
+        def _():
+            complete(same(step - 2))
+
+        @pl.when(has_other(step - 2))
+        def _():
+            complete(other(step - 2))
 
     load_w.wait()
     load_sel.wait()
@@ -209,15 +271,27 @@
         for relation, peer in enumerate((h_x, h_diag, h_core)):
             out_copy(group, peer, relation).wait()
 
-    @pl.loop(0, n_ctx - 1 - c)
+    @pl.when(side == 0)
+    def _():
+        pair_copy(c, h, 0, r1).wait_send()
+        pair_copy(c, h_x, 1, r2).wait_send()
+
+    @pl.loop(0, above)
     def _(step):
-        first_copy(c, n_ctx - 1 - step).wait_send()
+        first_copy(c, n_ctx - 2 + side - 2 * step).wait_send()
 
     @pl.loop(0, c)
     def _(source):
-        relay(source, h, h_x, s2, r2).wait_send()
         relay(source, h, h_core, s3, r3).wait_send()
         relay(source, h_x, h_core, s4, r4).wait_send()
+
+    @pl.loop(0, 2 * plane)
+    def _(source):
+        relay(source, h, h_x, s2, r2).wait_send()
+
+    @pl.loop(0, plane)
+    def _(lower):
+        side_copy(2 * lower + side).wait_send()
 
 
 def per_device(queries, latent_cache, selected, value_weight):
@@ -250,7 +324,7 @@
             pltpu.VMEM((scored_blocks, 2, GROUPS, KBLK, heads // GROUPS * KBLK), jnp.float32),
             pltpu.VMEM((heads, DC, DV), jnp.bfloat16),
             pltpu.VMEM((n_head, part, heads * DV), jnp.bfloat16),
-            dma((3,)),
+            dma((3,)), dma((2,)), dma((n_ctx,)),
             dma((n_ctx,)), dma((n_ctx,)),
             dma((n_ctx,)), dma((n_ctx,)),
             dma((n_ctx,)), dma((n_ctx,)),

time: 31.7 us -> 28.8 us (0.909)
  the two profiles are of different devices: /device:TPU:17 before, /device:TPU:25 now
where the time goes in v3:
time: 28.8 us; the launch traced here: 28.6 us
  Pallas kernels  26 us (90%)
  local copies, waits for them, and re-layouts  2.58 us (9%)
    pallas_call x1, Pallas kernels, per_device(): pl.pallas_call(functools.partial(kernel, n_ctx, n_head, heads, dense), ou...  26 us
    unnamed x3, local copies, waits for them, and re-layouts  1.47 us
    reshape x1, local copies, waits for them, and re-layouts, per_device(): own = latent_cache.reshape(tokens, width)  1.1 us

profile of v3, /device:TPU:25, one launch (start us, length us, event | category | flops | bytes accessed | tf_op | source)
XLA Modules:
  0.0 28.6 jit_solution(546158243013262884)
XLA Ops:
  0.0 1.1 %reshape.3.own_ref = bf16[128,576]{1,0:T(8,128)(2,1)S(1)} reshape(bf16[2,36864]{1,0:T(2,128)(2,1)} %param.5) | data formatting | bytes 294912 | tf_op jit(solution)/shard_map/reshape | solution.py:301
  1.1 0.0 copy-start
  1.1 0.7 %copy-done = s32[2,8]{1,0:T(2,128)S(1)} copy-done((s32[2,8]{1,0:T(2,128)S(1)}, s32[2,8]{1,0:T(2,128)}, u32[]{:S(2)}) %copy-start) | copy-done | bytes 88
  1.8 26.0 %shard_map.46 = bf16[32,8192]{1,0:T(8,128)(2,1)S(1)} custom-call(s32[2,8]{1,0:T(2,128)S(1)} %copy-done, bf16[128,576]{1,0:T(8,128)(2,1)S(1)} %reshape.3.own_ref, bf16[16,576,128]{2,1,0:T(8,128)(2,1)} %bitcast.1, bf16[16,512,128]{2,1,0:T(8,128)(2,1)} %w_hbm.1), custom_call_target="tpu_custom_call" | custom-call | tf_op jit(solution)/shard_map/pallas_call | solution.py:308
  27.8 0.8 %copy.6 = bf16[32,8192]{1,0:T(8,128)(2,1)} copy(bf16[32,8192]{1,0:T(8,128)(2,1)S(1)} %shard_map.46) | data formatting | bytes 1048576
Async XLA Ops:
  1.1 0.7 %copy-start = (s32[2,8]{1,0:T(2,128)S(1)}, s32[2,8]{1,0:T(2,128)}, u32[]{:S(2)}) copy-start(s32[2,8]{1,0:T(2,128)} %sel_hbm.1) | copy-start | bytes 196
